TPU v7x, 512 devices: a whole 4x4x16 slice. The times are simulated.
512 devices in a mesh: row: 16 (over z), col: 32 (over x, y, core).
Axes of the slice: x: 4, y: 4, z: 16, core: 2. Of those that a mesh axis runs over, the one named last changes fastest.
Arguments:
- level_one: bfloat16 [192, 262144], P(None, ('row', 'col')), may hold values from -6 to 6
- child_maps: bfloat16 [8, 192, 192], replicated, may hold values from -0.15625 to 0.15625
- translations: bfloat16 [32, 192, 192], replicated, may hold values from -0.078125 to 0.078125
- send_one: int32 [512, 32, 32], P(('row', 'col')), may hold values from 0 to 511
- list_one: int32 [262144, 32], P(('row', 'col')), may hold values from -1 to 1535, as said below
- send_two: int32 [512, 16, 16], P(('row', 'col')), may hold values from 0 to 63
- list_two: int32 [32768, 32], P(('row', 'col')), may hold values from -1 to 319, as said below
- list_three: int32 [4096, 32], P(('row', 'col')), may hold values from -1 to 255, as said below
Outputs:
- local_one: float32 [192, 262144], P(None, ('row', 'col'))
- local_two: float32 [192, 32768], P(None, ('row', 'col'))
- local_three: float32 [192, 4096], P(None, ('row', 'col'))
Inputs may be any that keep to these rules, and one draw needn't show every extreme that they name: `list_one`: -1 marks an offset without a source box. `list_two`: -1 marks an offset without a source box. `list_three`: -1 marks an offset without a source box.
All inputs are finite; a program needn't handle non-finite values.
Results may differ from a plain program's by a relative error of at most 0.0041.
Values may be sent and summed in bfloat16 or wider, within the bound.
A program may use at most 64 MiB of HBM per device.

v0:
```python
import jax
import jax.numpy as jnp
from jax import lax
from jax.sharding import PartitionSpec as P


def ascend(children, child_ops):
    parents = children.shape[1] // 8
    grouped = children.reshape(children.shape[0], parents, 8)
    summed = jnp.einsum("cde,ebc->db", child_ops, grouped, preferred_element_type=jnp.float32)
    return summed.astype(jnp.bfloat16)


def select_rows(table, entries, valid):
    clipped = jnp.clip(entries, 0, table.shape[0] - 1)
    picked = jnp.take(table, clipped, axis=0)
    return jnp.where(valid[:, :, None], picked, jnp.zeros_like(picked))


def apply_offsets(operators, picked):
    return jnp.einsum("ode,boe->bd", operators, picked, preferred_element_type=jnp.float32)


def on_device(
    level_one, child_maps, translations, send_one, list_one, send_two, list_two, list_three
):
    parents_two = ascend(level_one, child_maps)
    parents_three = ascend(parents_two, child_maps)
    table_one = level_one.T
    outgoing = jnp.take(table_one, send_one.reshape(-1), axis=0)
    arrived = lax.all_to_all(outgoing, "col", split_axis=0, concat_axis=0, tiled=True)
    buffer_one = jnp.concatenate([table_one, arrived], axis=0)
    local_one = apply_offsets(translations, select_rows(buffer_one, list_one, list_one >= 0)).T
    table_two = parents_two.T
    outgoing_two = jnp.take(table_two, send_two.reshape(-1), axis=0)
    arrived_two = lax.all_to_all(outgoing_two, "row", split_axis=0, concat_axis=0, tiled=True)
    buffer_two = jnp.concatenate([table_two, arrived_two], axis=0)
    local_two = (
        0.5 * apply_offsets(translations, select_rows(buffer_two, list_two, list_two >= 0)).T
    )
    table_three = parents_three.T
    count = table_three.shape[0]
    initial = jnp.zeros((count, list_three.shape[1], table_three.shape[1]), jnp.bfloat16)
    piece = lax.all_gather(table_three, "col", axis=0, tiled=True)
    valid = (list_three >= 0) & (list_three >= 0) & (list_three < piece.shape[0])
    clipped = jnp.clip(list_three, 0, piece.shape[0] - 1)
    rows_found = jnp.take(piece, clipped, axis=0)
    gathered = jnp.where(valid[:, :, None], rows_found, initial)
    local_three = 0.25 * apply_offsets(translations, gathered).T
    return (local_one, local_two, local_three)


def solution(mesh):
    placed = (
        P(None, ("row", "col")),
        P(),
        P(),
        P(("row", "col"), None, None),
        P(("row", "col"), None),
        P(("row", "col"), None, None),
        P(("row", "col"), None),
        P(("row", "col"), None),
    )
    return jax.shard_map(
        on_device,
        mesh=mesh,
        in_specs=placed,
        out_specs=(P(None, ("row", "col")), P(None, ("row", "col")), P(None, ("row", "col"))),
        check_vma=False,
    )
```

profile of v0, /device:TPU:1, one launch (start us, length us, event | category | flops | bytes accessed | tf_op | source)
XLA Modules:
  0.0 173.7 jit_solution(9117795894132228905)
XLA Ops:
  0.6 0.0 copy-start
  0.6 0.0 copy-start.4
  0.7 0.0 copy-start.3
  0.7 0.0 copy-start.6
  0.7 0.9 reshape.128
  1.6 0.7 compare_and_fusion.3
  2.3 1.1 copy.19
  3.4 0.0 copy-start.1
  3.5 1.6 fusion.12
  5.0 1.8 %gather_fusion.2 = bf16[256,192]{1,0:T(8,128)(2,1)} fusion(bf16[64,192]{1,0:T(8,128)(2,1)S(1)} %bitcast.57, s32[1024]{0:T(1024)S(1)} %pad_clamp_fusion.1), kind=kCustom, calls=%fused_computation.2 | custom fusion | bytes 197632 | tf_op jit(solution)/shard_map/jit(_take)/gather | solution.py:35
  6.8 1.7 broadcast_select_fusion.1
  8.5 15.8 %all-to-all-start.1 = ((bf16[16,16,192]{2,1,0:T(8,128)(2,1)}), bf16[16,16,192]{2,1,0:T(8,128)(2,1)}, u32[]{:S(2)}, u32[]{:S(2)}) async-start(bf16[16,16,192]{2,1,0:T(8,128)(2,1)} %broadcast_select_fusion.1), calls=%async_computation.1 | async-start | bytes 262144 | tf_op jit(solution)/shard_map/all_to_all | solution.py:36
  24.3 0.0 copy-done.4
  24.3 0.6 broadcast_compare_fusion.1
  24.9 0.0 copy-done.3
  24.9 0.7 reshape.125
  25.6 0.6 compare_and_fusion.2
  26.2 0.9 compare_select_fusion
  27.1 1.5 broadcast_compare_fusion
  28.6 0.0 copy-done.6
  28.6 0.6 compare_select_fusion.5
  29.2 0.6 compare_and_fusion.5
  29.7 0.1 copy.24
  29.8 0.1 reshape.156
  29.9 0.7 compare_select_fusion.3
  30.6 0.0 copy-start.5
  30.6 0.8 copy.20
  31.4 1.7 reshape.140
  33.1 0.8 broadcast_clamp_fusion
  34.0 0.0 copy-start.10
  34.0 0.0 copy-start.9
  34.0 1.4 fusion.15
  35.4 0.8 reshape.164
  36.2 4.9 %gather_fusion = bf16[1024,192]{1,0:T(8,128)(2,1)} fusion(bf16[512,192]{1,0:T(8,128)(2,1)S(1)} %bitcast.55, s32[1024]{0:T(1024)S(1)} %broadcast_clamp_fusion.2), kind=kCustom, calls=%fused_computation | custom fusion | bytes 790528 | tf_op jit(solution)/shard_map/jit(_take)/gather | solution.py:30
  41.2 0.0 copy-done.1
  41.2 0.0 copy-done.5
  41.2 2.1 %broadcast_select_fusion = bf16[32,32,192]{2,1,0:T(8,128)(2,1)} fusion(bf16[32,32,192]{2,1,0:T(8,128)(2,1)} %bitcast.61, pred[32,32]{1,0:T(8,128)(4,1)S(1)} %copy-done.5), kind=kLoop, calls=%fused_computation.30 | loop fusion | flops 196608 | bytes 787456 | tf_op jit(solution)/shard_map/jit(_take)/select_n | solution.py:30
  43.2 0.0 copy-done.10
  43.3 0.1 copy.26
  43.3 0.0 copy-done.9
  43.3 0.1 copy.27
  43.4 25.7 %all_gather.3 = bf16[256,192]{1,0:T(8,128)(2,1)S(1)} all-gather(bf16[8,192]{1,0:T(8,128)(2,1)S(1)} %fusion.15), channel_id=1, replica_groups=mesh['row'=16,'col'=32] {'col'}, dimensions={0}, use_global_device_ids=true | all-gather | bytes 101376 | tf_op jit(solution)/shard_map/all_gather | solution.py:44
  69.1 1.2 gather_fusion.4
  70.3 0.0 copy-done
  70.3 1.5 fusion.14
  71.8 0.0 all-to-all-done.1
  71.8 5.0 %all-to-all-start = ((bf16[32,32,192]{2,1,0:T(8,128)(2,1)}), bf16[32,32,192]{2,1,0:T(8,128)(2,1)}, u32[]{:S(2)}, u32[]{:S(2)}) async-start(bf16[32,32,192]{2,1,0:T(8,128)(2,1)} %broadcast_select_fusion), calls=%async_computation | async-start | bytes 1048576 | tf_op jit(solution)/shard_map/all_to_all | solution.py:31
  76.8 0.9 pad_maximum_fusion.1
  77.7 0.0 copy-start.11
  77.7 0.0 copy-start.12
  77.8 9.0 %gather_fusion.3 = bf16[2048,192]{1,0:T(8,128)(2,1)} fusion(bf16[320,192]{1,0:T(8,128)(2,1)S(1)} %pad_maximum_fusion.1, s32[2048]{0:T(1024)S(1)} %broadcast_clamp_fusion.1), kind=kCustom, calls=%fused_computation.3 | custom fusion | bytes 1581056 | tf_op jit(solution)/shard_map/jit(_take)/gather | solution.py:16
  86.8 0.0 copy-start.2
  86.8 0.0 copy-done.11
  86.8 0.0 copy-done.12
  86.8 3.5 %fusion.11 = f32[192,64]{0,1:T(8,128)} fusion(bf16[32,192,192]{2,1,0:T(8,128)(2,1)S(1)} %copy-done, bf16[64,32,192]{2,1,0:T(8,128)(2,1)} %bitcast.62, pred[64,32]{0,1:T(8,128)(4,1)S(1)} %copy-done.12, pred[64,32]{0,1:T(8,128)(4,1)S(1)} %copy-done.11), kind=kOutput, calls=%fused_computation.15 | convolution fusion | flops 151793664 | bytes 3198976 | tf_op jit(solution)/shard_map/ode,boe->bd/dot_general | solution.py:21
  90.3 0.0 all-to-all-done
  90.3 0.0 copy-done.2
  90.3 2.1 %pad_maximum_fusion = bf16[1536,192]{1,0:T(8,128)(2,1)} fusion(bf16[1024,192]{1,0:T(8,128)(2,1)} %bitcast.4, bf16[512,192]{1,0:T(8,128)(2,1)S(1)} %bitcast.56), kind=kLoop, calls=%fused_computation.27 | loop fusion | flops 1179648 | bytes 1179648 | tf_op jit(solution)/shard_map/concatenate | solution.py:32
  92.4 62.0 %gather_fusion.1 = bf16[16384,192]{1,0:T(8,128)(2,1)} fusion(bf16[1536,192]{1,0:T(8,128)(2,1)} %pad_maximum_fusion, s32[16384]{0:T(1024)S(1)} %broadcast_clamp_fusion), kind=kCustom, calls=%fused_computation.1 | custom fusion | bytes 12648448 | tf_op jit(solution)/shard_map/jit(_take)/gather | solution.py:16
  154.5 0.0 copy-start.8
  154.5 14.3 %copy.21 = bf16[512,32,192]{0,2,1:T(8,128)(2,1)} copy(bf16[512,32,192]{2,1,0:T(8,128)(2,1)} %bitcast.60) | data formatting | bytes 12582912 | tf_op jit(solution)/shard_map/jit(_take)/gather | solution.py:16
  168.7 0.0 copy-done.7
  168.7 0.0 copy-done.8
  168.7 5.0 %fusion.7 = f32[192,512]{1,0:T(8,128)} fusion(bf16[32,192,192]{2,1,0:T(8,128)(2,1)S(1)} %copy-done, bf16[512,32,192]{0,2,1:T(8,128)(2,1)} %copy.21, pred[512,32]{0,1:T(8,128)(4,1)S(1)} %copy-done.8, pred[512,32]{0,1:T(8,128)(4,1)S(1)} %copy-done.7), kind=kOutput, calls=%fused_computation.12 | convolution fusion | flops 1214251008 | bytes 9076736 | tf_op jit(solution)/shard_map/ode,boe->bd/dot_general | solution.py:21
  (7 shorter events, 0.0 us)
Async XLA Ops:
  0.6 69.7 %copy-start = (bf16[32,192,192]{2,1,0:T(8,128)(2,1)S(1)}, bf16[32,192,192]{2,1,0:T(8,128)(2,1)}, u32[]{:S(2)}) copy-start(bf16[32,192,192]{2,1,0:T(8,128)(2,1)} %param.10) | copy-start | bytes 7077892
  0.6 23.7 %copy-start.4 = (s32[64,32]{0,1:T(8,128)S(1)}, s32[64,32]{0,1:T(8,128)}, u32[]{:S(2)}) copy-start(s32[64,32]{0,1:T(8,128)} %param.14) | copy-start | bytes 24580
  0.7 24.3 %copy-start.3 = (s32[1,32,32]{2,1,0:T(8,128)S(1)}, s32[1,32,32]{2,1,0:T(8,128)}, u32[]{:S(2)}) copy-start(s32[1,32,32]{2,1,0:T(8,128)} %param.11) | copy-start | bytes 12292
  0.7 27.9 %copy-start.6 = (s32[8,32]{1,0:T(8,128)S(1)}, s32[8,32]{1,0:T(8,128)}, u32[]{:S(2)}) copy-start(s32[8,32]{1,0:T(8,128)} %param.15) | copy-start | bytes 3076
  3.4 37.8 %copy-start.1 = (bf16[192,512]{0,1:T(8,128)(2,1)}, bf16[192,512]{0,1:T(8,128)(2,1)S(1)}, u32[]{:S(2)}) copy-start(bf16[192,512]{0,1:T(8,128)(2,1)S(1)} %copy.19) | copy-start | bytes 589828
  8.5 63.3 %all-to-all-start.1 = ((bf16[16,16,192]{2,1,0:T(8,128)(2,1)}), bf16[16,16,192]{2,1,0:T(8,128)(2,1)}, u32[]{:S(2)}, u32[]{:S(2)}) async-start(bf16[16,16,192]{2,1,0:T(8,128)(2,1)} %broadcast_select_fusion.1), calls=%async_computation.1 | async-start | bytes 262144 | tf_op jit(solution)/shard_map/all_to_all | solution.py:36
  30.6 10.6 %copy-start.5 = (pred[32,32]{1,0:T(8,128)(4,1)S(1)}, pred[32,32]{1,0:T(8,128)(4,1)}, u32[]{:S(2)}) copy-start(pred[32,32]{1,0:T(8,128)(4,1)} %compare_and_fusion.2) | copy-start | bytes 3076
  34.0 9.3 %copy-start.10 = (pred[8,32]{1,0:T(8,128)(4,1)S(1)}, pred[8,32]{1,0:T(8,128)(4,1)}, u32[]{:S(2)}) copy-start(pred[8,32]{1,0:T(8,128)(4,1)} %get-tuple-element.7) | copy-start | bytes 772
  34.0 9.3 %copy-start.9 = (pred[8,32]{1,0:T(8,128)(4,1)S(1)}, pred[8,32]{1,0:T(8,128)(4,1)}, u32[]{:S(2)}) copy-start(pred[8,32]{1,0:T(8,128)(4,1)} %get-tuple-element.8) | copy-start | bytes 772
  71.8 18.4 %all-to-all-start = ((bf16[32,32,192]{2,1,0:T(8,128)(2,1)}), bf16[32,32,192]{2,1,0:T(8,128)(2,1)}, u32[]{:S(2)}, u32[]{:S(2)}) async-start(bf16[32,32,192]{2,1,0:T(8,128)(2,1)} %broadcast_select_fusion), calls=%async_computation | async-start | bytes 1048576 | tf_op jit(solution)/shard_map/all_to_all | solution.py:31
  77.7 9.0 %copy-start.11 = (pred[64,32]{0,1:T(8,128)(4,1)S(1)}, pred[64,32]{0,1:T(8,128)(4,1)}, u32[]{:S(2)}) copy-start(pred[64,32]{0,1:T(8,128)(4,1)} %get-tuple-element.5) | copy-start | bytes 6148
  77.7 9.0 %copy-start.12 = (pred[64,32]{0,1:T(8,128)(4,1)S(1)}, pred[64,32]{0,1:T(8,128)(4,1)}, u32[]{:S(2)}) copy-start(pred[64,32]{0,1:T(8,128)(4,1)} %get-tuple-element.6) | copy-start | bytes 6148
  86.8 3.5 %copy-start.2 = (bf16[192,512]{0,1:T(8,128)(2,1)S(1)}, bf16[192,512]{0,1:T(8,128)(2,1)}, u32[]{:S(2)}) copy-start(bf16[192,512]{0,1:T(8,128)(2,1)} %copy-done.1) | copy-start | bytes 589828
  154.4 14.3 %copy-start.7 = (pred[512,32]{0,1:T(8,128)(4,1)S(1)}, pred[512,32]{0,1:T(8,128)(4,1)}, u32[]{:S(2)}) copy-start(pred[512,32]{0,1:T(8,128)(4,1)} %get-tuple-element.3) | copy-start | bytes 49156
  154.5 14.3 %copy-start.8 = (pred[512,32]{0,1:T(8,128)(4,1)S(1)}, pred[512,32]{0,1:T(8,128)(4,1)}, u32[]{:S(2)}) copy-start(pred[512,32]{0,1:T(8,128)(4,1)} %get-tuple-element.4) | copy-start | bytes 49156
where the time goes:
time: 175 us; the launch traced here: 174 us
  local copies, waits for them, and re-layouts  99.6 us (57%)
  blocking collectives  25.7 us (15%)
  starting transfers between devices  20.7 us (12%)
  other arithmetic  13.9 us (8%)
  matrix products  13 us (7%)
    gather x3, local copies, waits for them, and re-layouts, select_rows(): picked = jnp.take(table, clipped, axis=0)  85.3 us
    all_gather x1, blocking collectives, on_device(): piece = lax.all_gather(table_three, 'col', axis=0, tiled=True)  25.7 us
    all_to_all x1, starting transfers between devices, on_device(): lax.all_to_all(outgoing_two, 'row', split_axis=0, concat_axis=0, tiled=True)  15.8 us
    dot_general x3, matrix products, apply_offsets(): jnp.einsum('ode,boe->bd', operators, picked, preferred_element_type=jnp.f...  10 us
    all_to_all x1, starting transfers between devices, on_device(): lax.all_to_all(outgoing, 'col', split_axis=0, concat_axis=0, tiled=True)  4.96 us
    gather x1, local copies, waits for them, and re-layouts, on_device(): outgoing = jnp.take(table_one, send_one.reshape(-1), axis=0)  4.94 us
  transfers between devices with their start and end apart: 2, of which 0 were waited for; matrix products, arithmetic and copies ran while one was open for 20% of the time, Pallas kernels for 0%

commit v1 on v0

v1 whole, which is shorter than its diff:
```python
import jax
import jax.numpy as jnp
from jax import lax
from jax.experimental import pallas as pl
from jax.experimental.pallas import tpu as pltpu
from jax.sharding import PartitionSpec as P

BF = jnp.bfloat16
F32 = jnp.float32
NT = (((1,), (1,)), ((), ()))
D, NOFF, B1, B2, B3 = 192, 32, 512, 64, 8
NCOL, NROW, GH1, GH2 = 32, 16, 32, 16
MESH = pl.DeviceIdType.MESH


def iota(shape, axis):
    return lax.broadcasted_iota(jnp.int32, shape, axis)


def dot(a, b):
    return jnp.dot(a, b, preferred_element_type=F32)


def dot_nt(a, b):
    return lax.dot_general(a, b, NT, preferred_element_type=F32)


def hot(mask):
    return jnp.where(mask, 1.0, 0.0).astype(BF)


def turned(table):
    eye = hot(iota((D, D), 0) == iota((D, D), 1))
    return dot_nt(eye, table).astype(BF)


def kernel(
    one_ref, send1_ref, list1_ref, send2_ref, list2_ref, list3_ref, maps_hbm, trans_hbm,
    out1_ref, out2_ref, out3_ref,
    maps, trans, tcat, send1, ghost1, send2, ghost2, send3, ghost3, g1, g23, tab1,
    load_sem, send_sem, recv_sem,
):
    row = lax.axis_index("row")
    col = lax.axis_index("col")
    load_maps = pltpu.make_async_copy(maps_hbm, maps, load_sem.at[0])
    load_trans = pltpu.make_async_copy(trans_hbm, trans, load_sem.at[1])
    load_maps.start()
    load_trans.start()

    barrier = pltpu.get_barrier_semaphore()

    def hello_col(i, _):
        pl.semaphore_signal(barrier, inc=1, device_id=(row, (col + i) % NCOL), device_id_type=MESH)
        return 0

    def hello_row(i, _):
        pl.semaphore_signal(barrier, inc=1, device_id=((row + i) % NROW, col), device_id_type=MESH)
        return 0

    lax.fori_loop(1, NCOL, hello_col, 0)
    lax.fori_loop(1, NROW, hello_row, 0)

    who = send1_ref[...].T
    lane = iota((GH1, B1), 1)
    for p0 in range(0, NCOL, 8):
        pick = jnp.concatenate([hot(who[:, p : p + 1] == lane) for p in range(p0, p0 + 8)], axis=0)
        rows = dot_nt(pick, one_ref[...]).astype(BF)
        send1[p0 : p0 + 8] = rows.reshape(8, GH1, D)
    ghost1[col] = send1[col]

    pl.semaphore_wait(barrier, NCOL - 1 + NROW - 1)

    def to_col1(i):
        peer = (col + i) % NCOL
        return pltpu.make_async_remote_copy(
            src_ref=send1.at[peer], dst_ref=ghost1.at[col], send_sem=send_sem.at[0],
            recv_sem=recv_sem.at[0], device_id=(row, peer), device_id_type=MESH)

    def to_row2(i):
        peer = (row + i) % NROW
        return pltpu.make_async_remote_copy(
            src_ref=send2.at[peer], dst_ref=ghost2.at[row], send_sem=send_sem.at[1],
            recv_sem=recv_sem.at[1], device_id=(peer, col), device_id_type=MESH)

    def to_col3(i):
        peer = (col + i) % NCOL
        return pltpu.make_async_remote_copy(
            src_ref=send3, dst_ref=ghost3.at[col], send_sem=send_sem.at[2],
            recv_sem=recv_sem.at[2], device_id=(row, peer), device_id_type=MESH)

    def start(copy):
        def step(i, _):
            copy(i).start()
            return 0
        return step

    lax.fori_loop(1, NCOL, start(to_col1), 0)

    load_maps.wait()
    r = iota((B1, B1), 0)
    pick = hot(iota((B1, B1), 1) == (r & (B2 - 1)) * 8 + (r >> 6))
    children = dot_nt(pick, one_ref[...]).astype(BF)
    total = jnp.zeros((B2, D), F32)
    for c in range(8):
        total = total + dot_nt(children[c * B2 : (c + 1) * B2], maps[c])
    two = total.astype(BF)
    who = send2_ref[...].T
    lane = iota((GH2, B2), 1)
    pick = jnp.concatenate([hot(who[:, p : p + 1] == lane) for p in range(NROW)], axis=0)
    send2[...] = dot(pick, two).astype(BF).reshape(NROW, GH2, D)
    ghost2[row] = send2[row]
    lax.fori_loop(1, NROW, start(to_row2), 0)

    r = iota((128, B2), 0)
    pick = hot(iota((128, B2), 1) == (r & 15) * 8 + (r >> 4))
    children = dot(pick, two).astype(BF)
    total = jnp.zeros((16, D), F32)
    for c in range(8):
        total = total + dot_nt(children[c * 16 : (c + 1) * 16], maps[c])
    three = total.astype(BF)
    send3[...] = three
    ghost3[col] = three
    lax.fori_loop(1, NCOL, start(to_col3), 0)

    def own(o, _):
        pick = hot(iota((B1, B1), 0) == list1_ref[pl.ds(o, 1), :])
        g1[pl.ds(pl.multiple_of(o * D, D), D), :] = dot(one_ref[...], pick).astype(BF)
        return 0

    lax.fori_loop(0, NOFF, own, 0, unroll=2)

    load_trans.wait()
    for o in range(0, NOFF, 2):
        tcat[:, o * D : (o + 2) * D] = jnp.concatenate([trans[o], trans[o + 1]], axis=1)

    pltpu.make_async_copy(ghost1.at[0 : NCOL - 1], ghost1.at[0 : NCOL - 1], recv_sem.at[0]).wait()
    tab1[...] = turned(ghost1[...].reshape(NCOL * GH1, D))

    def far(o, _):
        pick = hot(iota((NCOL * GH1, B1), 0) == list1_ref[pl.ds(o, 1), :] - B1)
        at = pl.ds(pl.multiple_of(o * D, D), D)
        g1[at, :] = g1[at, :] + dot(tab1[...], pick).astype(BF)
        return 0

    lax.fori_loop(0, NOFF, far, 0, unroll=2)
    out1_ref[...] = dot(tcat[...], g1[...])

    pltpu.make_async_copy(ghost2.at[0 : NROW - 1], ghost2.at[0 : NROW - 1], recv_sem.at[1]).wait()
    tab2 = turned(jnp.concatenate([two, ghost2[...].reshape(NROW * GH2, D)], axis=0))
    list2 = list2_ref[...]
    g23[...] = jnp.zeros_like(g23)
    for o in range(0, NOFF, 4):
        entries = jnp.concatenate([list2[o + j : o + j + 1, :] for j in range(4)], axis=1)
        pick = hot(iota((B2 + NROW * GH2, 4 * B2), 0) == entries)
        found = dot(tab2, pick).astype(BF)
        for j in range(4):
            g23[(o + j) * D : (o + j + 1) * D, 0:B2] = found[:, j * B2 : (j + 1) * B2]

    pltpu.make_async_copy(ghost3.at[0 : NCOL - 1], ghost3.at[0 : NCOL - 1], recv_sem.at[2]).wait()
    tab3 = turned(ghost3[...].reshape(NCOL * 16, D))
    spread = hot(iota((NOFF, NOFF * B3), 1) // B3 == iota((NOFF, NOFF * B3), 0))
    wide = dot(list3_ref[...].astype(F32).astype(BF), spread)
    keep = iota((B3, NOFF * B3), 1) % B3 == iota((B3, NOFF * B3), 0)
    entries = jnp.sum(jnp.where(keep, wide, 0.0), axis=0, keepdims=True).astype(jnp.int32)
    entries = entries + (entries & -8)
    pick = hot(iota((NCOL * 16, NOFF * B3), 0) == entries)
    found = dot(tab3, pick).astype(BF)
    for o in range(NOFF):
        g23[o * D : (o + 1) * D, B2 : B2 + B3] = found[:, o * B3 : (o + 1) * B3]
    both = dot(tcat[...], g23[...])
    both = both.T
    out2_ref[...] = 0.5 * both[0:B2]
    out3_ref[...] = 0.25 * both[B2 : B2 + B3]

    pltpu.make_async_copy(send1.at[0 : NCOL - 1], send1.at[0 : NCOL - 1], send_sem.at[0]).wait()
    pltpu.make_async_copy(send2.at[0 : NROW - 1], send2.at[0 : NROW - 1], send_sem.at[1]).wait()
    pltpu.make_async_copy(ghost3.at[0 : NCOL - 1], ghost3.at[0 : NCOL - 1], send_sem.at[2]).wait()


def on_device(
    level_one, child_maps, translations, send_one, list_one, send_two, list_two, list_three
):
    vmem = pl.BlockSpec(memory_space=pltpu.VMEM)
    any_ = pl.BlockSpec(memory_space=pl.ANY)
    out1, out2, out3 = pl.pallas_call(
        kernel,
        out_shape=(
            jax.ShapeDtypeStruct((D, B1), F32),
            jax.ShapeDtypeStruct((B2, D), F32),
            jax.ShapeDtypeStruct((B3, D), F32),
        ),
        in_specs=[vmem] * 6 + [any_] * 2,
        out_specs=(vmem, vmem, vmem),
        scratch_shapes=[
            pltpu.VMEM((8, D, D), BF),
            pltpu.VMEM((NOFF, D, D), BF),
            pltpu.VMEM((D, NOFF * D), BF),
            pltpu.VMEM((NCOL, GH1, D), BF),
            pltpu.VMEM((NCOL, GH1, D), BF),
            pltpu.VMEM((NROW, GH2, D), BF),
            pltpu.VMEM((NROW, GH2, D), BF),
            pltpu.VMEM((16, D), BF),
            pltpu.VMEM((NCOL, 16, D), BF),
            pltpu.VMEM((NOFF * D, B1), BF),
            pltpu.VMEM((NOFF * D, 128), BF),
            pltpu.VMEM((D, NCOL * GH1), BF),
            pltpu.SemaphoreType.DMA((2,)),
            pltpu.SemaphoreType.DMA((3,)),
            pltpu.SemaphoreType.DMA((3,)),
        ],
        compiler_params=pltpu.CompilerParams(
            collective_id=0, has_side_effects=True, vmem_limit_bytes=60 << 20
        ),
    )(
        level_one, send_one.reshape(NCOL, GH1), list_one.T, send_two.reshape(NROW, GH2),
        list_two.T, list_three, child_maps, translations,
    )
    return out1, out2.T, out3.T


def solution(mesh):
    placed = (
        P(None, ("row", "col")),
        P(),
        P(),
        P(("row", "col"), None, None),
        P(("row", "col"), None),
        P(("row", "col"), None, None),
        P(("row", "col"), None),
        P(("row", "col"), None),
    )
    return jax.shard_map(
        on_device,
        mesh=mesh,
        in_specs=placed,
        out_specs=(P(None, ("row", "col")), P(None, ("row", "col")), P(None, ("row", "col"))),
        check_vma=False,
    )
```

time: 175 us -> 48.5 us (0.28)
  local copies, waits for them, and re-layouts: 99.6 us -> 4.53 us
  Pallas kernels: 0 us -> 43.1 us
  blocking collectives: 25.7 us -> 0 us
  starting transfers between devices: 20.7 us -> 0 us
  other arithmetic: 13.9 us -> 0 us
  matrix products: 13 us -> 0 us
    gather x6 -> x0, local copies, waits for them, and re-layouts: 93.2 us -> none  [the longest x3 85.3 us: select_rows(): picked = jnp.take(table, clipped, axis=0)]
    pallas_call x0 -> x1, Pallas kernels: none -> 43.1 us  [on_device(): pl.pallas_call(kernel, out_shape=(jax.ShapeDtypeStruct((D, B1), F32), jax...]
    all_gather x1 -> x0, blocking collectives: 25.7 us -> none  [on_device(): piece = lax.all_gather(table_three, 'col', axis=0, tiled=True)]
    all_to_all x2 -> x0, starting transfers between devices: 20.7 us -> none  [the longest x1 15.8 us: on_device(): lax.all_to_all(outgoing_two, 'row', split_axis=0, concat_axis=0, tiled=True)]
    dot_general x5 -> x0, matrix products: 13 us -> none  [the longest x3 10 us: apply_offsets(): jnp.einsum('ode,boe->bd', operators, picked, preferred_element_type=jnp.f...]
    select_n x7 -> x0, other arithmetic: 5.89 us -> none  [the longest x2 2.76 us: on_device(): outgoing = jnp.take(table_one, send_one.reshape(-1), axis=0)]
    unnamed x27 -> x3, local copies, waits for them, and re-layouts: 1.12 us -> 4.53 us
    concatenate x2 -> x0, other arithmetic: 3.07 us -> none  [the longest x1 2.14 us: on_device(): buffer_one = jnp.concatenate([table_one, arrived], axis=0)]
  transfers between devices with their start and end apart: 2 -> 0, of which waited for: 0 -> 0; matrix products, arithmetic and copies ran while one was open for 20% -> 0% of each run, Pallas kernels for 0% -> 0%
where the time goes in v1:
time: 48.5 us; the launch traced here: 48.2 us
  Pallas kernels  43.1 us (89%)
  local copies, waits for them, and re-layouts  4.53 us (9%)
  between operations  0.64 us (1%)
    pallas_call x1, Pallas kernels, on_device(): pl.pallas_call(kernel, out_shape=(jax.ShapeDtypeStruct((D, B1), F32), jax...  43.1 us
    unnamed x3, local copies, waits for them, and re-layouts  4.53 us

profile of v1, /device:TPU:1, one launch (start us, length us, event | category | flops | bytes accessed | tf_op | source)
XLA Modules:
  0.0 48.2 jit_solution(12774502321407018496)
XLA Ops:
  0.6 43.1 %shard_map.103 = (f32[192,512]{1,0:T(8,128)}, f32[64,192]{1,0:T(8,128)}, f32[8,192]{1,0:T(8,128)}) custom-call(bf16[192,512]{1,0:T(8,128)(2,1)} %one_ref.1, s32[32,32]{1,0:T(8,128)} %bitcast.8, s32[32,512]{1,0:T(8,128)} %bitcast.6, s32[16,16]{1,0:T(8,128)} %bitcast.10, s32[32,64]{1,0:T(8,128)} %bitcast.9, s32[8,32]{1,0:T(8,128)} %list3_ref.1, ...), custom_call_target="tpu_custom_call" | custom-call | tf_op jit(solution)/shard_map/pallas_call | solution.py:185
  43.7 1.8 %copy.14 = f32[192,512]{1,0:T(8,128)} copy(f32[192,512]{1,0:T(8,128)} %get-tuple-element.12) | data formatting | bytes 786432
  45.5 1.5 %copy.15 = f32[192,64]{0,1:T(8,128)} copy(f32[192,64]{0,1:T(8,128)} %bitcast.7) | data formatting | bytes 98304
  47.0 1.3 %copy.16 = f32[192,8]{0,1:T(8,128)} copy(f32[192,8]{0,1:T(8,128)} %bitcast.11) | data formatting | bytes 12288

commit v2 on v1

v2 whole, which is shorter than its diff:
```python
import jax
import jax.numpy as jnp
from jax import lax
from jax.experimental import pallas as pl
from jax.experimental.pallas import tpu as pltpu
from jax.sharding import PartitionSpec as P

BF = jnp.bfloat16
F32 = jnp.float32
NT = (((1,), (1,)), ((), ()))
D, NOFF, B1, B2, B3 = 192, 32, 512, 64, 8
NCOL, NROW, GH1, GH2 = 32, 16, 32, 16
ROWS = B2 + NROW
SLAB, WIDE = 128, 256
MESH = pl.DeviceIdType.MESH


def iota(shape, axis):
    return lax.broadcasted_iota(jnp.int32, shape, axis)


def dot(a, b):
    return jnp.dot(a, b, preferred_element_type=F32)


def dot_nt(a, b):
    return lax.dot_general(a, b, NT, preferred_element_type=F32)


def hot(mask):
    return jnp.where(mask, 1.0, 0.0).astype(BF)


def turned(table):
    eye = hot(iota((D, D), 0) == iota((D, D), 1))
    return dot_nt(eye, table).astype(BF)


def upward(one_ref, maps, send2_ref, table_ref, three_ref):
    r = iota((B1, B1), 0)
    pick = hot(iota((B1, B1), 1) == (r & (B2 - 1)) * 8 + (r >> 6))
    children = dot_nt(pick, one_ref[...]).astype(BF)
    total = jnp.zeros((B2, D), F32)
    for c in range(8):
        total = total + dot_nt(children[c * B2 : (c + 1) * B2], maps[c])
    two = total.astype(BF)
    table_ref[...] = jnp.zeros_like(table_ref)
    table_ref[0:B2, 0:D] = two
    spread = hot(iota((NROW, D), 0) == iota((NROW, D), 1))
    table_ref[B2:ROWS, 0:D] = dot(send2_ref[...].astype(F32).astype(BF), spread).astype(BF)
    r = iota((128, B2), 0)
    pick = hot(iota((128, B2), 1) == (r & 15) * 8 + (r >> 4))
    children = dot(pick, two).astype(BF)
    total = jnp.zeros((16, D), F32)
    for c in range(8):
        total = total + dot_nt(children[c * 16 : (c + 1) * 16], maps[c])
    three_ref[...] = total.astype(BF)


def plane(
    one_hbm, send1_ref, list1_hbm, list3_ref, three_ref, trans_hbm,
    out1_ref, out3_ref,
    one_ref, list1_ref, trans, tcat, send1, ghost1, ghost3, g1, g3, tab1,
    load_sem, send_sem, recv_sem,
):
    row = lax.axis_index("row")
    col = lax.axis_index("col")
    load_one = pltpu.make_async_copy(one_hbm, one_ref, load_sem.at[0])
    load_list = pltpu.make_async_copy(list1_hbm, list1_ref, load_sem.at[1])
    load_trans = pltpu.make_async_copy(trans_hbm, trans, load_sem.at[2])
    load_one.start()
    load_list.start()
    load_trans.start()

    barrier = pltpu.get_barrier_semaphore()

    def hello(i, _):
        pl.semaphore_signal(barrier, inc=1, device_id=(row, (col + i) % NCOL), device_id_type=MESH)
        return 0

    lax.fori_loop(1, NCOL, hello, 0)

    who = send1_ref[...].T
    lane = iota((GH1, B1), 1)
    load_one.wait()
    for p0 in range(0, NCOL, 8):
        pick = jnp.concatenate([hot(who[:, p : p + 1] == lane) for p in range(p0, p0 + 8)], axis=0)
        rows = dot_nt(pick, one_ref[...]).astype(BF)
        send1[p0 : p0 + 8] = rows.reshape(8, GH1, D)
    ghost1[col] = send1[col]
    ghost3[col] = three_ref[...]

    pl.semaphore_wait(barrier, NCOL - 1)

    def to_col1(i):
        peer = (col + i) % NCOL
        return pltpu.make_async_remote_copy(
            src_ref=send1.at[peer], dst_ref=ghost1.at[col], send_sem=send_sem.at[0],
            recv_sem=recv_sem.at[0], device_id=(row, peer), device_id_type=MESH)

    def to_col3(i):
        peer = (col + i) % NCOL
        return pltpu.make_async_remote_copy(
            src_ref=three_ref, dst_ref=ghost3.at[col], send_sem=send_sem.at[1],
            recv_sem=recv_sem.at[1], device_id=(row, peer), device_id_type=MESH)

    def start(copy):
        def step(i, _):
            copy(i).start()
            return 0
        return step

    lax.fori_loop(1, NCOL, start(to_col1), 0)
    lax.fori_loop(1, NCOL, start(to_col3), 0)

    load_list.wait()

    def own(o, _):
        pick = hot(iota((B1, B1), 0) == list1_ref[pl.ds(o, 1), :])
        g1[pl.ds(pl.multiple_of(o * D, D), D), :] = dot(one_ref[...], pick).astype(BF)
        return 0

    lax.fori_loop(0, NOFF, own, 0, unroll=2)

    load_trans.wait()
    for o in range(0, NOFF, 2):
        tcat[:, o * D : (o + 2) * D] = jnp.concatenate([trans[o], trans[o + 1]], axis=1)

    pltpu.make_async_copy(ghost3.at[0 : NCOL - 1], ghost3.at[0 : NCOL - 1], recv_sem.at[1]).wait()
    tab3 = turned(ghost3[...].reshape(NCOL * 16, D))
    spread = hot(iota((NOFF, NOFF * B3), 1) // B3 == iota((NOFF, NOFF * B3), 0))
    wide = dot(list3_ref[...].astype(F32).astype(BF), spread)
    keep = iota((B3, NOFF * B3), 1) % B3 == iota((B3, NOFF * B3), 0)
    entries = jnp.sum(jnp.where(keep, wide, 0.0), axis=0, keepdims=True).astype(jnp.int32)
    entries = entries + (entries & -8)
    pick = hot(iota((NCOL * 16, NOFF * B3), 0) == entries)
    found = dot(tab3, pick).astype(BF)
    g3[...] = jnp.zeros_like(g3)
    for o in range(NOFF):
        g3[o * D : (o + 1) * D, 0:B3] = found[:, o * B3 : (o + 1) * B3]
    out3_ref[...] = 0.25 * dot(tcat[...], g3[...]).T[0:B3]

    pltpu.make_async_copy(ghost1.at[0 : NCOL - 1], ghost1.at[0 : NCOL - 1], recv_sem.at[0]).wait()
    tab1[...] = turned(ghost1[...].reshape(NCOL * GH1, D))

    def far(o, _):
        pick = hot(iota((NCOL * GH1, B1), 0) == list1_ref[pl.ds(o, 1), :] - B1)
        at = pl.ds(pl.multiple_of(o * D, D), D)
        g1[at, :] = g1[at, :] + dot(tab1[...], pick).astype(BF)
        return 0

    lax.fori_loop(0, NOFF, far, 0, unroll=2)
    out1_ref[...] = dot(tcat[...], g1[...])

    pltpu.make_async_copy(ghost1.at[0 : NCOL - 1], ghost1.at[0 : NCOL - 1], send_sem.at[0]).wait()
    pltpu.make_async_copy(ghost3.at[0 : NCOL - 1], ghost3.at[0 : NCOL - 1], send_sem.at[1]).wait()


def across(
    table_ref, list2_ref, out1_in, out3_in, trans_hbm, out1_ref, out2_ref, out3_ref, trans, sem,
):
    row = lax.axis_index("row")
    pass1 = pltpu.make_async_copy(out1_in, out1_ref, sem.at[0])
    load_trans = pltpu.make_async_copy(trans_hbm, trans, sem.at[1])
    load_trans.start()
    pass1.start()
    out3_ref[...] = out3_in[...]

    table = table_ref[:, 0:ROWS, 0:D].reshape(NROW * ROWS, D)
    every = turned(table)
    mine = hot(iota((NROW, NROW * ROWS), 1) == iota((NROW, NROW * ROWS), 0) * ROWS + B2 + row)
    sent = dot(mine, table)[:, 0:GH2].astype(BF)
    ghosts = NROW * GH2
    spread = hot(iota((NROW, ghosts), 1) // GH2 == iota((NROW, ghosts), 0))
    wide = lax.dot_general(sent, spread, (((0,), (0,)), ((), ())), preferred_element_type=F32)
    keep = iota((GH2, ghosts), 1) % GH2 == iota((GH2, ghosts), 0)
    local = jnp.sum(jnp.where(keep, wide, 0.0), axis=0, keepdims=True).astype(jnp.int32)
    source = local + iota((1, ghosts), 1) // GH2 * ROWS
    pick = hot(iota((NROW * ROWS, ghosts), 0) == source)
    far = dot(every, pick).astype(BF)
    pick = hot(iota((NROW * ROWS, B2), 0) == iota((NROW * ROWS, B2), 1) + row * ROWS)
    near = dot(every, pick).astype(BF)

    list2 = list2_ref[...]
    load_trans.wait()
    total = jnp.zeros((D, B2), F32)
    for o in range(0, NOFF, 4):
        entries = jnp.concatenate([list2[o + j : o + j + 1, :] for j in range(4)], axis=1)
        found = dot(near, hot(iota((B2, 4 * B2), 0) == entries))
        found = found + dot(far, hot(iota((ghosts, 4 * B2), 0) == entries - B2))
        found = found.astype(BF)
        for j in range(4):
            total = total + dot(trans[o + j], found[:, j * B2 : (j + 1) * B2])
    out2_ref[...] = 0.5 * total.T
    pass1.wait()


def on_device(
    level_one, child_maps, translations, send_one, list_one, send_two, list_two, list_three
):
    vmem = pl.BlockSpec(memory_space=pltpu.VMEM)
    any_ = pl.BlockSpec(memory_space=pl.ANY)
    table, three = pl.pallas_call(
        upward,
        out_shape=(jax.ShapeDtypeStruct((SLAB, WIDE), BF), jax.ShapeDtypeStruct((16, D), BF)),
        in_specs=[vmem] * 3,
        out_specs=(vmem, vmem),
    )(level_one, child_maps, send_two.reshape(NROW, GH2))
    tables = lax.all_gather(table, "row", axis=0, tiled=True)
    out1, out3 = pl.pallas_call(
        plane,
        out_shape=(jax.ShapeDtypeStruct((D, B1), F32), jax.ShapeDtypeStruct((B3, D), F32)),
        in_specs=[any_, vmem, any_, vmem, vmem, any_],
        out_specs=(vmem, vmem),
        scratch_shapes=[
            pltpu.VMEM((D, B1), BF),
            pltpu.VMEM((NOFF, B1), jnp.int32),
            pltpu.VMEM((NOFF, D, D), BF),
            pltpu.VMEM((D, NOFF * D), BF),
            pltpu.VMEM((NCOL, GH1, D), BF),
            pltpu.VMEM((NCOL, GH1, D), BF),
            pltpu.VMEM((NCOL, 16, D), BF),
            pltpu.VMEM((NOFF * D, B1), BF),
            pltpu.VMEM((NOFF * D, 128), BF),
            pltpu.VMEM((D, NCOL * GH1), BF),
            pltpu.SemaphoreType.DMA((3,)),
            pltpu.SemaphoreType.DMA((2,)),
            pltpu.SemaphoreType.DMA((2,)),
        ],
        compiler_params=pltpu.CompilerParams(
            collective_id=0, has_side_effects=True, vmem_limit_bytes=60 << 20
        ),
        cost_estimate=pl.CostEstimate(
            flops=2 * NOFF * D * B1 * (3 * B1 + D), bytes_accessed=4 << 20, transcendentals=0
        ),
    )(
        level_one, send_one.reshape(NCOL, GH1), list_one.T, list_three, three, translations,
    )
    out1, out2, out3 = pl.pallas_call(
        across,
        out_shape=(
            jax.ShapeDtypeStruct((D, B1), F32),
            jax.ShapeDtypeStruct((B2, D), F32),
            jax.ShapeDtypeStruct((B3, D), F32),
        ),
        in_specs=[vmem, vmem, any_, vmem, any_],
        out_specs=(any_, vmem, vmem),
        scratch_shapes=[pltpu.VMEM((NOFF, D, D), BF), pltpu.SemaphoreType.DMA((2,))],
        compiler_params=pltpu.CompilerParams(vmem_limit_bytes=60 << 20),
    )(tables.reshape(NROW, SLAB, WIDE), list_two.T, out1, out3, translations)
    return out1, out2.T, out3.T


def solution(mesh):
    placed = (
        P(None, ("row", "col")),
        P(),
        P(),
        P(("row", "col"), None, None),
        P(("row", "col"), None),
        P(("row", "col"), None, None),
        P(("row", "col"), None),
        P(("row", "col"), None),
    )
    return jax.shard_map(
        on_device,
        mesh=mesh,
        in_specs=placed,
        out_specs=(P(None, ("row", "col")), P(None, ("row", "col")), P(None, ("row", "col"))),
        check_vma=False,
    )
```

time: 48.5 us -> 108 us (2.23)
  the two profiles are of different devices: /device:TPU:1 before, /device:TPU:6 now
where the time goes in v2:
time: 108 us
  Pallas kernels  51.8 us (48%)
  waiting for transfers between devices  42.2 us (39%)
  between operations  14.1 us (13%)
    all_gather x1, waiting for transfers between devices, on_device(): tables = lax.all_gather(table, 'row', axis=0, tiled=True)  42.1 us
    pallas_call x1, Pallas kernels, on_device(): pl.pallas_call(plane, out_shape=(jax.ShapeDtypeStruct((D, B1), F32), jax....  33.8 us
    pallas_call x1, Pallas kernels, on_device(): pl.pallas_call(across, out_shape=(jax.ShapeDtypeStruct((D, B1), F32), jax...  14.9 us
    pallas_call x1, Pallas kernels, on_device(): pl.pallas_call(upward, out_shape=(jax.ShapeDtypeStruct((SLAB, WIDE), BF),...  3.07 us
  transfers between devices with their start and end apart: 1, of which 1 were waited for; matrix products, arithmetic and copies ran while one was open for 0% of the time, Pallas kernels for 31%

profile of v2, /device:TPU:6, one launch (start us, length us, event | category | flops | bytes accessed | tf_op | source)
XLA Modules:
  0.0 108.1 jit_solution(6478453117453964939)
XLA Ops:
  7.2 0.0 all-gather.2.cloned.1.call-start
  7.2 3.1 %shard_map.103 = (bf16[128,256]{1,0:T(8,128)(2,1)}, bf16[16,192]{1,0:T(8,128)(2,1)}) custom-call(bf16[192,512]{1,0:T(8,128)(2,1)} %one_hbm.1, bf16[8,192,192]{2,1,0:T(8,128)(2,1)} %maps.1, s32[16,16]{1,0:T(8,128)} %bitcast.9), custom_call_target="tpu_custom_call" | custom-call | tf_op jit(solution)/shard_map/pallas_call | solution.py:203
  10.3 0.0 all-gather.2.cloned.1.call-update
  10.3 33.8 %shard_map.104 = (f32[192,512]{1,0:T(8,128)}, f32[8,192]{1,0:T(8,128)}) custom-call(bf16[192,512]{1,0:T(8,128)(2,1)} %one_hbm.1, s32[32,32]{1,0:T(8,128)} %bitcast.12, s32[32,512]{1,0:T(8,128)} %bitcast.10, s32[8,32]{1,0:T(8,128)} %list3_ref.1, bf16[16,192]{1,0:T(8,128)(2,1)} %get-tuple-element.11.three_ref, bf16[32,192,192]{2,1,0:T(8,128)(2,1)} %trans_hbm.3), custom_call_target="tpu_custom_call" | custom-call | flops 10871635968 | bytes 4194304 | tf_op jit(solution)/shard_map/pallas_call | solution.py:210
  44.2 42.1 %all-gather.2.cloned.1.call-done = bf16[2048,256]{1,0:T(8,128)(2,1)} async-done(((bf16[128,256]{1,0:T(8,128)(2,1)}), bf16[2048,256]{1,0:T(8,128)(2,1)}) %all-gather.2.cloned.1.call-update) | async-done | bytes 1048592 | tf_op jit(solution)/shard_map/all_gather | solution.py:209
  86.3 14.9 %shard_map.105 = (f32[192,512]{1,0:T(8,128)}, f32[64,192]{1,0:T(8,128)}, f32[8,192]{1,0:T(8,128)}) custom-call(bf16[16,128,256]{2,1,0:T(8,128)(2,1)} %bitcast.7, s32[32,64]{1,0:T(8,128)} %bitcast.8, f32[192,512]{1,0:T(8,128)} %get-tuple-element.12.out1_in, f32[8,192]{1,0:T(8,128)} %get-tuple-element.13.out3_in, bf16[32,192,192]{2,1,0:T(8,128)(2,1)} %trans_hbm.3), custom_call_target="tpu_custom_call" | custom-call | tf_op jit(solution)/shard_map/pallas_call | solution.py:239
Async XLA Ops:
  7.2 79.1 %all-gather.2.cloned.1.call-start = ((), (), s32[]{:S(2)}) async-start(), calls=%async_computation | async-start | bytes 1114112 | tf_op jit(solution)/shard_map/all_gather | solution.py:209
Sparse Core Ops, SparseCore 0:
  10.7 75.6 all-gather.1

commit v3 on v1

v3 whole, which is shorter than its diff:
```python
import jax
import jax.numpy as jnp
from jax import lax
from jax.experimental import pallas as pl
from jax.experimental.pallas import tpu as pltpu
from jax.sharding import PartitionSpec as P

BF = jnp.bfloat16
F32 = jnp.float32
NT = (((1,), (1,)), ((), ()))
D, NOFF, B1, B2, B3 = 192, 32, 512, 64, 8
NCOL, NROW, GH1, GH2 = 32, 16, 32, 16
PACK = 48
MESSAGE = PACK + 2 * B3
MESH = pl.DeviceIdType.MESH


def iota(shape, axis):
    return lax.broadcasted_iota(jnp.int32, shape, axis)


def dot(a, b):
    return jnp.dot(a, b, preferred_element_type=F32)


def dot_nt(a, b):
    return lax.dot_general(a, b, NT, preferred_element_type=F32)


def hot(mask):
    return jnp.where(mask, 1.0, 0.0).astype(BF)


def turned(table):
    w = table.shape[1]
    eye = hot(iota((w, w), 0) == iota((w, w), 1))
    return dot_nt(eye, table).astype(BF)


def as_row(entries, width):
    k, p = entries.shape
    n = p * width
    spread = hot(iota((p, n), 1) // width == iota((p, n), 0))
    wide = dot(entries.astype(F32).astype(BF), spread)
    keep = iota((k, n), 1) % width == iota((k, n), 0)
    return jnp.sum(jnp.where(keep, wide, 0.0), axis=0, keepdims=True).astype(jnp.int32)


def kernel(
    one_hbm, send1_ref, list1_hbm, send2_ref, list2_ref, list3_ref, maps_hbm, trans_hbm,
    out1_ref, out2_ref, out3_ref,
    one_ref, list1_ref, maps, trans, tcat, send1, ghost1, send2, ghost2, g, tab1,
    load_sem, send_sem, recv_sem,
):
    row = lax.axis_index("row")
    col = lax.axis_index("col")
    barrier = pltpu.get_barrier_semaphore()

    def hello_col(i, _):
        pl.semaphore_signal(barrier, inc=1, device_id=(row, lax.rem(col + i, NCOL)), device_id_type=MESH)
        return 0

    def hello_row(i, _):
        pl.semaphore_signal(barrier, inc=1, device_id=(lax.rem(row + i, NROW), col), device_id_type=MESH)
        return 0

    load_one = pltpu.make_async_copy(one_hbm, one_ref, load_sem.at[0])
    load_one.start()
    load_maps = pltpu.make_async_copy(maps_hbm, maps, load_sem.at[1])
    load_maps.start()
    lax.fori_loop(1, NROW, hello_row, 0)
    lax.fori_loop(1, NCOL, hello_col, 0)
    load_list = pltpu.make_async_copy(list1_hbm, list1_ref, load_sem.at[2])
    load_trans = pltpu.make_async_copy(trans_hbm, trans, load_sem.at[3])
    load_list.start()
    load_trans.start()

    who = send1_ref[...].T
    lane = iota((GH1, B1), 1)
    load_one.wait()
    for p0 in range(0, NCOL, 8):
        pick = jnp.concatenate([hot(who[:, p : p + 1] == lane) for p in range(p0, p0 + 8)], axis=0)
        rows = dot_nt(pick, one_ref[...]).reshape(8, GH1, D)
        send1[p0 : p0 + 8, 0:GH1] = rows[:, :, 0:128].astype(BF)
        rest = rows[:, :, 128:D]
        rest = jnp.concatenate([rest[:, 0 : GH1 // 2], rest[:, GH1 // 2 :]], axis=2)
        send1[p0 : p0 + 8, GH1:PACK] = rest.astype(BF)
    load_maps.wait()
    r = iota((B1, B1), 0)
    pick = hot(iota((B1, B1), 1) == (r & (B2 - 1)) * 8 + (r >> 6))
    children = dot_nt(pick, one_ref[...]).astype(BF)
    total = jnp.zeros((B2, D), F32)
    for c in range(8):
        total = total + dot_nt(children[c * B2 : (c + 1) * B2], maps[c])
    two = total.astype(BF)
    who = send2_ref[...].T
    lane = iota((GH2, B2), 1)
    pick = jnp.concatenate([hot(who[:, p : p + 1] == lane) for p in range(NROW)], axis=0)
    send2[...] = dot(pick, two).astype(BF).reshape(NROW, GH2, D)
    ghost2[row] = send2[row]

    r = iota((128, B2), 0)
    pick = hot(iota((128, B2), 1) == (r & 15) * 8 + (r >> 4))
    children = dot(pick, two).astype(BF)
    total = jnp.zeros((16, D), F32)
    for c in range(8):
        total = total + dot_nt(children[c * 16 : (c + 1) * 16], maps[c])
    rest = jnp.concatenate([total[0:B3, 128:D], jnp.zeros((B3, 256 - D), F32)], axis=1)
    three = jnp.concatenate([total[0:B3, 0:128], rest], axis=0).astype(BF)
    send1[:, PACK:MESSAGE] = jnp.broadcast_to(three[None], (NCOL, 2 * B3, 128))
    ghost1[col] = send1[col]

    pl.semaphore_wait(barrier, NCOL - 1 + NROW - 1)

    def to_col1(i):
        peer = lax.rem(col + i, NCOL)
        return pltpu.make_async_remote_copy(
            src_ref=send1.at[peer], dst_ref=ghost1.at[col], send_sem=send_sem.at[0],
            recv_sem=recv_sem.at[0], device_id=(row, peer), device_id_type=MESH)

    def to_row2(i):
        peer = lax.rem(row + i, NROW)
        return pltpu.make_async_remote_copy(
            src_ref=send2.at[peer], dst_ref=ghost2.at[row], send_sem=send_sem.at[1],
            recv_sem=recv_sem.at[1], device_id=(peer, col), device_id_type=MESH)

    def start(copy):
        def step(i, _):
            copy(i).start()
            return 0
        return step

    lax.fori_loop(1, NCOL, start(to_col1), 0)
    lax.fori_loop(1, NROW, start(to_row2), 0)

    load_list.wait()

    def own(o, _):
        pick = hot(iota((B1, B1), 0) == list1_ref[pl.ds(o, 1), :])
        g[pl.ds(pl.multiple_of(o * D, D), D), 0:B1] = dot(one_ref[...], pick).astype(BF)
        return 0

    lax.fori_loop(0, NOFF, own, 0, unroll=8)

    load_trans.wait()
    for o in range(0, NOFF, 2):
        tcat[:, o * D : (o + 2) * D] = jnp.concatenate([trans[o], trans[o + 1]], axis=1)

    list2 = list2_ref[...]
    entries3 = as_row(list3_ref[...], B3)
    entries3 = entries3 + (entries3 & -8)
    pltpu.make_async_copy(ghost2.at[0 : NROW - 1], ghost2.at[0 : NROW - 1], recv_sem.at[1]).wait()
    tab2 = turned(jnp.concatenate([two, ghost2[...].reshape(NROW * GH2, D)], axis=0))
    g[:, B1:] = jnp.zeros((NOFF * D, 128), BF)
    for o in range(0, NOFF, 4):
        entries = jnp.concatenate([list2[o + j : o + j + 1, :] for j in range(4)], axis=1)
        pick = hot(iota((B2 + NROW * GH2, 4 * B2), 0) == entries)
        found = dot(tab2, pick).astype(BF)
        for j in range(4):
            g[(o + j) * D : (o + j + 1) * D, B1 : B1 + B2] = found[:, j * B2 : (j + 1) * B2]

    there = list1_ref[...] - B1
    there = jnp.where(
        there >= 0, ((there >> 4) & 1) * B1 + (there >> 5) * (GH1 // 2) + (there & 15), -1
    )
    list1_ref[...] = there
    pltpu.make_async_copy(ghost1.at[0 : NCOL - 1], ghost1.at[0 : NCOL - 1], recv_sem.at[0]).wait()
    half = GH1 // 2
    tab1[0:128, 0:B1] = turned(ghost1[:, 0:half].reshape(B1, 128))
    tab1[0:128, B1:] = turned(ghost1[:, half:GH1].reshape(B1, 128))
    rest = turned(ghost1[:, GH1:PACK].reshape(B1, 128))
    tab1[128:D, 0:B1] = rest[0 : D - 128]
    tab1[128:D, B1:] = rest[D - 128 :]

    tab3 = turned(ghost1[:, PACK:MESSAGE].reshape(NCOL * 16, 128))
    place = iota((NCOL * 16, NOFF * B3), 0)
    low = dot(tab3, hot(place == entries3))
    high = dot(tab3[0 : D - 128], hot(place == entries3 + 8))
    found = jnp.concatenate([low, high], axis=0).astype(BF)
    for o in range(NOFF):
        g[o * D : (o + 1) * D, B1 + B2 : B1 + B2 + B3] = found[:, o * B3 : (o + 1) * B3]

    def far(o, _):
        pick = hot(iota((NCOL * GH1, B1), 0) == list1_ref[pl.ds(o, 1), :])
        at = pl.ds(pl.multiple_of(o * D, D), D)
        g[at, 0:B1] = g[at, 0:B1] + dot(tab1[...], pick).astype(BF)
        return 0

    lax.fori_loop(0, NOFF, far, 0, unroll=8)
    total = dot(tcat[...], g[...])
    out1_ref[...] = total[:, 0:B1]
    both = total[:, B1:].T
    out2_ref[...] = 0.5 * both[0:B2]
    out3_ref[...] = 0.25 * both[B2 : B2 + B3]

    pltpu.make_async_copy(send1.at[0 : NCOL - 1], send1.at[0 : NCOL - 1], send_sem.at[0]).wait()
    pltpu.make_async_copy(send2.at[0 : NROW - 1], send2.at[0 : NROW - 1], send_sem.at[1]).wait()


def pass_on(*refs):
    for source, target in zip(refs[0:3], refs[3:6]):
        target[...] = source[...]


def on_device(
    level_one, child_maps, translations, send_one, list_one, send_two, list_two, list_three
):
    vmem = pl.BlockSpec(memory_space=pltpu.VMEM)
    any_ = pl.BlockSpec(memory_space=pl.ANY)
    shapes = (
        jax.ShapeDtypeStruct((D, B1), F32),
        jax.ShapeDtypeStruct((B2, D), F32),
        jax.ShapeDtypeStruct((B3, D), F32),
    )
    found = pl.pallas_call(
        kernel,
        out_shape=shapes,
        in_specs=[any_, vmem, any_, vmem, vmem, vmem, any_, any_],
        out_specs=(vmem, vmem, vmem),
        scratch_shapes=[
            pltpu.VMEM((D, B1), BF),
            pltpu.VMEM((NOFF, B1), jnp.int32),
            pltpu.VMEM((8, D, D), BF),
            pltpu.VMEM((NOFF, D, D), BF),
            pltpu.VMEM((D, NOFF * D), BF),
            pltpu.VMEM((NCOL, MESSAGE, 128), BF),
            pltpu.VMEM((NCOL, MESSAGE, 128), BF),
            pltpu.VMEM((NROW, GH2, D), BF),
            pltpu.VMEM((NROW, GH2, D), BF),
            pltpu.VMEM((NOFF * D, B1 + 128), BF),
            pltpu.VMEM((D, NCOL * GH1), BF),
            pltpu.SemaphoreType.DMA((4,)),
            pltpu.SemaphoreType.DMA((2,)),
            pltpu.SemaphoreType.DMA((2,)),
        ],
        compiler_params=pltpu.CompilerParams(
            collective_id=0, has_side_effects=True, vmem_limit_bytes=60 << 20
        ),
    )(
        level_one, send_one.reshape(NCOL, GH1), list_one.T, send_two.reshape(NROW, GH2),
        list_two.T, list_three, child_maps, translations,
    )
    out1, out2, out3 = pl.pallas_call(
        pass_on,
        out_shape=shapes,
        in_specs=[vmem] * 3,
        out_specs=(vmem,) * 3,
    )(*found)
    return out1, out2.T, out3.T


def solution(mesh):
    placed = (
        P(None, ("row", "col")),
        P(),
        P(),
        P(("row", "col"), None, None),
        P(("row", "col"), None),
        P(("row", "col"), None, None),
        P(("row", "col"), None),
        P(("row", "col"), None),
    )
    return jax.shard_map(
        on_device,
        mesh=mesh,
        in_specs=placed,
        out_specs=(P(None, ("row", "col")), P(None, ("row", "col")), P(None, ("row", "col"))),
        check_vma=False,
    )
```

time: 48.5 us -> 43.6 us (0.90)
  local copies, waits for them, and re-layouts: 4.53 us -> 0 us
    unnamed x3 -> x0, local copies, waits for them, and re-layouts: 4.53 us -> none
    pallas_call x1 -> x2, Pallas kernels: 43.1 us -> 42.8 us  [the longest x1 40.9 us: on_device(): pl.pallas_call(kernel, out_shape=shapes, in_specs=[any_, vmem, any_, vmem...]
where the time goes in v3:
time: 43.6 us; the launch traced here: 43.4 us
  Pallas kernels  42.8 us (98%)
  between operations  0.64 us (1%)
    pallas_call x1, Pallas kernels, on_device(): pl.pallas_call(kernel, out_shape=shapes, in_specs=[any_, vmem, any_, vmem...  40.9 us
    pallas_call x1, Pallas kernels, on_device(): pl.pallas_call(pass_on, out_shape=shapes, in_specs=[vmem] * 3, out_specs=...  1.82 us

profile of v3, /device:TPU:1, one launch (start us, length us, event | category | flops | bytes accessed | tf_op | source)
XLA Modules:
  0.0 43.4 jit_solution(3783910276609071834)
XLA Ops:
  0.6 40.9 %shard_map.103 = (f32[192,512]{1,0:T(8,128)}, f32[64,192]{1,0:T(8,128)}, f32[8,192]{1,0:T(8,128)}) custom-call(bf16[192,512]{1,0:T(8,128)(2,1)} %one_hbm.1, s32[32,32]{1,0:T(8,128)} %bitcast.7, s32[32,512]{1,0:T(8,128)} %bitcast.6, s32[16,16]{1,0:T(8,128)} %bitcast.9, s32[32,64]{1,0:T(8,128)} %bitcast.8, s32[8,32]{1,0:T(8,128)} %list3_ref.1, ...), custom_call_target="tpu_custom_call" | custom-call | tf_op jit(solution)/shard_map/pallas_call | solution.py:215
  41.6 1.8 %shard_map.104 = (f32[192,512]{1,0:T(8,128)}, f32[64,192]{1,0:T(8,128)}, f32[8,192]{1,0:T(8,128)}) custom-call(f32[192,512]{1,0:T(8,128)} %get-tuple-element.9.refs_0_, f32[64,192]{1,0:T(8,128)} %get-tuple-element.10.refs_1_, f32[8,192]{1,0:T(8,128)} %get-tuple-element.11.refs_2_), custom_call_target="tpu_custom_call" | custom-call | tf_op jit(solution)/shard_map/pallas_call | solution.py:243

commit v4 on v3

--- a/solution.py
+++ b/solution.py
@@ -10,6 +10,8 @@
 NT = (((1,), (1,)), ((), ()))
 D, NOFF, B1, B2, B3 = 192, 32, 512, 64, 8
 NCOL, NROW, GH1, GH2 = 32, 16, 32, 16
+GROUP = 8
+CHUNK = 8
 PACK = 48
 MESSAGE = PACK + 2 * B3
 MESH = pl.DeviceIdType.MESH
@@ -50,26 +52,28 @@
     one_hbm, send1_ref, list1_hbm, send2_ref, list2_ref, list3_ref, maps_hbm, trans_hbm,
     out1_ref, out2_ref, out3_ref,
     one_ref, list1_ref, maps, trans, tcat, send1, ghost1, send2, ghost2, g, tab1,
-    load_sem, send_sem, recv_sem,
+    load_sem, send_sem, recv_sem, plane_sem, all_sem,
 ):
     row = lax.axis_index("row")
     col = lax.axis_index("col")
     barrier = pltpu.get_barrier_semaphore()
 
-    def hello_col(i, _):
-        pl.semaphore_signal(barrier, inc=1, device_id=(row, lax.rem(col + i, NCOL)), device_id_type=MESH)
-        return 0
-
-    def hello_row(i, _):
-        pl.semaphore_signal(barrier, inc=1, device_id=(lax.rem(row + i, NROW), col), device_id_type=MESH)
+    gate = lax.rem(col, GROUP) == 0
+
+    def hello(i, _):
+        peer = lax.rem(col + i, NCOL)
+
+        @pl.when(lax.rem(peer, GROUP) != 0)
+        def _():
+            pl.semaphore_signal(barrier, inc=1, device_id=(row, peer), device_id_type=MESH)
+
         return 0
 
     load_one = pltpu.make_async_copy(one_hbm, one_ref, load_sem.at[0])
     load_one.start()
     load_maps = pltpu.make_async_copy(maps_hbm, maps, load_sem.at[1])
     load_maps.start()
-    lax.fori_loop(1, NROW, hello_row, 0)
-    lax.fori_loop(1, NCOL, hello_col, 0)
+    lax.fori_loop(1, NCOL, hello, 0)
     load_list = pltpu.make_async_copy(list1_hbm, list1_ref, load_sem.at[2])
     load_trans = pltpu.make_async_copy(trans_hbm, trans, load_sem.at[3])
     load_list.start()
@@ -110,7 +114,27 @@
     send1[:, PACK:MESSAGE] = jnp.broadcast_to(three[None], (NCOL, 2 * B3, 128))
     ghost1[col] = send1[col]
 
-    pl.semaphore_wait(barrier, NCOL - 1 + NROW - 1)
+    @pl.when(jnp.logical_not(gate))
+    def _():
+        pl.semaphore_wait(barrier, NCOL - 1)
+
+        def tell(q, _):
+            pl.semaphore_signal(plane_sem, inc=1, device_id=(row, q * GROUP), device_id_type=MESH)
+            return 0
+
+        lax.fori_loop(0, NCOL // GROUP, tell, 0)
+
+    @pl.when(gate)
+    def _():
+        pl.semaphore_wait(plane_sem, NCOL - NCOL // GROUP)
+
+        def tell(i, _):
+            pl.semaphore_signal(
+                barrier, inc=1, device_id=(lax.rem(row + i, NROW), col), device_id_type=MESH
+            )
+            return 0
+
+        lax.fori_loop(1, NROW, tell, 0)
 
     def to_col1(i):
         peer = lax.rem(col + i, NCOL)
@@ -131,7 +155,6 @@
         return step
 
     lax.fori_loop(1, NCOL, start(to_col1), 0)
-    lax.fori_loop(1, NROW, start(to_row2), 0)
 
     load_list.wait()
 
@@ -149,15 +172,7 @@
     list2 = list2_ref[...]
     entries3 = as_row(list3_ref[...], B3)
     entries3 = entries3 + (entries3 & -8)
-    pltpu.make_async_copy(ghost2.at[0 : NROW - 1], ghost2.at[0 : NROW - 1], recv_sem.at[1]).wait()
-    tab2 = turned(jnp.concatenate([two, ghost2[...].reshape(NROW * GH2, D)], axis=0))
     g[:, B1:] = jnp.zeros((NOFF * D, 128), BF)
-    for o in range(0, NOFF, 4):
-        entries = jnp.concatenate([list2[o + j : o + j + 1, :] for j in range(4)], axis=1)
-        pick = hot(iota((B2 + NROW * GH2, 4 * B2), 0) == entries)
-        found = dot(tab2, pick).astype(BF)
-        for j in range(4):
-            g[(o + j) * D : (o + j + 1) * D, B1 : B1 + B2] = found[:, j * B2 : (j + 1) * B2]
 
     there = list1_ref[...] - B1
     there = jnp.where(
@@ -186,10 +201,46 @@
         g[at, 0:B1] = g[at, 0:B1] + dot(tab1[...], pick).astype(BF)
         return 0
 
-    lax.fori_loop(0, NOFF, far, 0, unroll=8)
-    total = dot(tcat[...], g[...])
-    out1_ref[...] = total[:, 0:B1]
-    both = total[:, B1:].T
+    def across():
+        @pl.when(gate)
+        def _():
+            pl.semaphore_wait(barrier, NROW - 1)
+
+            def tell(i, _):
+                pl.semaphore_signal(all_sem, inc=1, device_id=(row, col + i), device_id_type=MESH)
+                return 0
+
+            lax.fori_loop(1, GROUP, tell, 0)
+
+        @pl.when(jnp.logical_not(gate))
+        def _():
+            pl.semaphore_wait(all_sem, 1)
+
+        lax.fori_loop(1, NROW, start(to_row2), 0)
+
+    place = jnp.maximum(2 - row // 4, 0)
+
+    def chunk(n, _):
+        pl.when(n == place)(across)
+
+        def step(k, _):
+            return far(n * CHUNK + k, 0)
+
+        return lax.fori_loop(0, CHUNK, step, 0, unroll=True)
+
+    lax.fori_loop(0, NOFF // CHUNK, chunk, 0)
+    out1_ref[...] = dot(tcat[...], g[:, 0:B1])
+
+    pltpu.make_async_copy(ghost2.at[0 : NROW - 1], ghost2.at[0 : NROW - 1], recv_sem.at[1]).wait()
+    tab2 = turned(jnp.concatenate([two, ghost2[...].reshape(NROW * GH2, D)], axis=0))
+    for o in range(0, NOFF, 4):
+        entries = jnp.concatenate([list2[o + j : o + j + 1, :] for j in range(4)], axis=1)
+        pick = hot(iota((B2 + NROW * GH2, 4 * B2), 0) == entries)
+        found = dot(tab2, pick).astype(BF)
+        for j in range(4):
+            g[(o + j) * D : (o + j + 1) * D, B1 : B1 + B2] = found[:, j * B2 : (j + 1) * B2]
+
+    both = dot(tcat[...], g[:, B1:]).T
     out2_ref[...] = 0.5 * both[0:B2]
     out3_ref[...] = 0.25 * both[B2 : B2 + B3]
 
@@ -232,6 +283,8 @@
             pltpu.SemaphoreType.DMA((4,)),
             pltpu.SemaphoreType.DMA((2,)),
             pltpu.SemaphoreType.DMA((2,)),
+            pltpu.SemaphoreType.REGULAR,
+            pltpu.SemaphoreType.REGULAR,
         ],
         compiler_params=pltpu.CompilerParams(
             collective_id=0, has_side_effects=True, vmem_limit_bytes=60 << 20

time: 43.6 us -> 39.7 us (0.911)
  Pallas kernels: 42.8 us -> 38.5 us
    pallas_call x1, Pallas kernels: 40.9 us -> 36.7 us  [on_device(): pl.pallas_call(kernel, out_shape=shapes, in_specs=[any_, vmem, any_, vmem...]
where the time goes in v4:
time: 39.7 us; the launch traced here: 39.2 us
  Pallas kernels  38.5 us (97%)
  between operations  0.64 us (2%)
    pallas_call x1, Pallas kernels, on_device(): pl.pallas_call(kernel, out_shape=shapes, in_specs=[any_, vmem, any_, vmem...  36.7 us
    pallas_call x1, Pallas kernels, on_device(): pl.pallas_call(pass_on, out_shape=shapes, in_specs=[vmem] * 3, out_specs=...  1.82 us

profile of v4, /device:TPU:1, one launch (start us, length us, event | category | flops | bytes accessed | tf_op | source)
XLA Modules:
  0.0 39.2 jit_solution(14716888340998203522)
XLA Ops:
  0.6 36.7 %shard_map.103 = (f32[192,512]{1,0:T(8,128)}, f32[64,192]{1,0:T(8,128)}, f32[8,192]{1,0:T(8,128)}) custom-call(bf16[192,512]{1,0:T(8,128)(2,1)} %one_hbm.1, s32[32,32]{1,0:T(8,128)} %bitcast.7, s32[32,512]{1,0:T(8,128)} %bitcast.6, s32[16,16]{1,0:T(8,128)} %bitcast.9, s32[32,64]{1,0:T(8,128)} %bitcast.8, s32[8,32]{1,0:T(8,128)} %list3_ref.1, ...), custom_call_target="tpu_custom_call" | custom-call | tf_op jit(solution)/shard_map/pallas_call | solution.py:266
  37.3 1.8 %shard_map.104 = (f32[192,512]{1,0:T(8,128)}, f32[64,192]{1,0:T(8,128)}, f32[8,192]{1,0:T(8,128)}) custom-call(f32[192,512]{1,0:T(8,128)} %get-tuple-element.9.refs_0_, f32[64,192]{1,0:T(8,128)} %get-tuple-element.10.refs_1_, f32[8,192]{1,0:T(8,128)} %get-tuple-element.11.refs_2_), custom_call_target="tpu_custom_call" | custom-call | tf_op jit(solution)/shard_map/pallas_call | solution.py:296

commit v5 on v4

--- a/solution.py
+++ b/solution.py
@@ -12,6 +12,7 @@
 NCOL, NROW, GH1, GH2 = 32, 16, 32, 16
 GROUP = 8
 CHUNK = 8
+SLOTS = NOFF // CHUNK
 PACK = 48
 MESSAGE = PACK + 2 * B3
 MESH = pl.DeviceIdType.MESH
@@ -89,6 +90,17 @@
         rest = rows[:, :, 128:D]
         rest = jnp.concatenate([rest[:, 0 : GH1 // 2], rest[:, GH1 // 2 :]], axis=2)
         send1[p0 : p0 + 8, GH1:PACK] = rest.astype(BF)
+
+    @pl.when(jnp.logical_not(gate))
+    def _():
+        pl.semaphore_wait(barrier, NCOL - 1)
+
+        def tell(q, _):
+            pl.semaphore_signal(plane_sem, inc=1, device_id=(row, q * GROUP), device_id_type=MESH)
+            return 0
+
+        lax.fori_loop(0, NCOL // GROUP, tell, 0)
+
     load_maps.wait()
     r = iota((B1, B1), 0)
     pick = hot(iota((B1, B1), 1) == (r & (B2 - 1)) * 8 + (r >> 6))
@@ -114,16 +126,6 @@
     send1[:, PACK:MESSAGE] = jnp.broadcast_to(three[None], (NCOL, 2 * B3, 128))
     ghost1[col] = send1[col]
 
-    @pl.when(jnp.logical_not(gate))
-    def _():
-        pl.semaphore_wait(barrier, NCOL - 1)
-
-        def tell(q, _):
-            pl.semaphore_signal(plane_sem, inc=1, device_id=(row, q * GROUP), device_id_type=MESH)
-            return 0
-
-        lax.fori_loop(0, NCOL // GROUP, tell, 0)
-
     @pl.when(gate)
     def _():
         pl.semaphore_wait(plane_sem, NCOL - NCOL // GROUP)
@@ -156,6 +158,36 @@
 
     lax.fori_loop(1, NCOL, start(to_col1), 0)
 
+    def across():
+        @pl.when(gate)
+        def _():
+            pl.semaphore_wait(barrier, NROW - 1)
+
+            def tell(i, _):
+                pl.semaphore_signal(all_sem, inc=1, device_id=(row, col + i), device_id_type=MESH)
+                return 0
+
+            lax.fori_loop(1, GROUP, tell, 0)
+
+        @pl.when(jnp.logical_not(gate))
+        def _():
+            pl.semaphore_wait(all_sem, 1)
+
+        lax.fori_loop(1, NROW, start(to_row2), 0)
+
+    turn = jnp.where(row < 4, 5, 3)
+
+    def chunks(work, before):
+        def chunk(n, _):
+            pl.when(n + before == turn)(across)
+
+            def step(k, _):
+                return work(n * CHUNK + k, 0)
+
+            return lax.fori_loop(0, CHUNK, step, 0, unroll=True)
+
+        return chunk
+
     load_list.wait()
 
     def own(o, _):
@@ -163,7 +195,7 @@
         g[pl.ds(pl.multiple_of(o * D, D), D), 0:B1] = dot(one_ref[...], pick).astype(BF)
         return 0
 
-    lax.fori_loop(0, NOFF, own, 0, unroll=8)
+    lax.fori_loop(0, SLOTS, chunks(own, 0), 0)
 
     load_trans.wait()
     for o in range(0, NOFF, 2):
@@ -201,34 +233,7 @@
         g[at, 0:B1] = g[at, 0:B1] + dot(tab1[...], pick).astype(BF)
         return 0
 
-    def across():
-        @pl.when(gate)
-        def _():
-            pl.semaphore_wait(barrier, NROW - 1)
-
-            def tell(i, _):
-                pl.semaphore_signal(all_sem, inc=1, device_id=(row, col + i), device_id_type=MESH)
-                return 0
-
-            lax.fori_loop(1, GROUP, tell, 0)
-
-        @pl.when(jnp.logical_not(gate))
-        def _():
-            pl.semaphore_wait(all_sem, 1)
-
-        lax.fori_loop(1, NROW, start(to_row2), 0)
-
-    place = jnp.maximum(2 - row // 4, 0)
-
-    def chunk(n, _):
-        pl.when(n == place)(across)
-
-        def step(k, _):
-            return far(n * CHUNK + k, 0)
-
-        return lax.fori_loop(0, CHUNK, step, 0, unroll=True)
-
-    lax.fori_loop(0, NOFF // CHUNK, chunk, 0)
+    lax.fori_loop(0, SLOTS, chunks(far, SLOTS), 0)
     out1_ref[...] = dot(tcat[...], g[:, 0:B1])
 
     pltpu.make_async_copy(ghost2.at[0 : NROW - 1], ghost2.at[0 : NROW - 1], recv_sem.at[1]).wait()

time: 39.7 us -> 36.8 us (0.927)
  Pallas kernels: 38.5 us -> 36 us
    pallas_call x1, Pallas kernels: 36.7 us -> 34.1 us  [on_device(): pl.pallas_call(kernel, out_shape=shapes, in_specs=[any_, vmem, any_, vmem...]
where the time goes in v5:
time: 36.8 us; the launch traced here: 36.6 us
  Pallas kernels  36 us (98%)
  between operations  0.64 us (2%)
    pallas_call x1, Pallas kernels, on_device(): pl.pallas_call(kernel, out_shape=shapes, in_specs=[any_, vmem, any_, vmem...  34.1 us
    pallas_call x1, Pallas kernels, on_device(): pl.pallas_call(pass_on, out_shape=shapes, in_specs=[vmem] * 3, out_specs=...  1.82 us

profile of v5, /device:TPU:1, one launch (start us, length us, event | category | flops | bytes accessed | tf_op | source)
XLA Modules:
  0.0 36.6 jit_solution(11088137419092131453)
XLA Ops:
  0.6 34.1 %shard_map.103 = (f32[192,512]{1,0:T(8,128)}, f32[64,192]{1,0:T(8,128)}, f32[8,192]{1,0:T(8,128)}) custom-call(bf16[192,512]{1,0:T(8,128)(2,1)} %one_hbm.1, s32[32,32]{1,0:T(8,128)} %bitcast.7, s32[32,512]{1,0:T(8,128)} %bitcast.6, s32[16,16]{1,0:T(8,128)} %bitcast.9, s32[32,64]{1,0:T(8,128)} %bitcast.8, s32[8,32]{1,0:T(8,128)} %list3_ref.1, ...), custom_call_target="tpu_custom_call" | custom-call | tf_op jit(solution)/shard_map/pallas_call | solution.py:271
  34.8 1.8 %shard_map.104 = (f32[192,512]{1,0:T(8,128)}, f32[64,192]{1,0:T(8,128)}, f32[8,192]{1,0:T(8,128)}) custom-call(f32[192,512]{1,0:T(8,128)} %get-tuple-element.9.refs_0_, f32[64,192]{1,0:T(8,128)} %get-tuple-element.10.refs_1_, f32[8,192]{1,0:T(8,128)} %get-tuple-element.11.refs_2_), custom_call_target="tpu_custom_call" | custom-call | tf_op jit(solution)/shard_map/pallas_call | solution.py:301

commit v6 on v5

--- a/solution.py
+++ b/solution.py
@@ -50,10 +50,10 @@
 
 
 def kernel(
-    one_hbm, send1_ref, list1_hbm, send2_ref, list2_ref, list3_ref, maps_hbm, trans_hbm,
+    one_hbm, send1_hbm, list1_hbm, send2_hbm, list2_hbm, list3_hbm, maps_hbm, trans_hbm,
     out1_ref, out2_ref, out3_ref,
     one_ref, list1_ref, maps, trans, tcat, send1, ghost1, send2, ghost2, g, tab1,
-    load_sem, send_sem, recv_sem, plane_sem, all_sem,
+    send1_ref, send2_ref, list2_ref, list3_ref, far1, load_sem, send_sem, recv_sem, plane_sem, all_sem,
 ):
     row = lax.axis_index("row")
     col = lax.axis_index("col")
@@ -72,6 +72,14 @@
 
     load_one = pltpu.make_async_copy(one_hbm, one_ref, load_sem.at[0])
     load_one.start()
+    load_send1 = pltpu.make_async_copy(send1_hbm, send1_ref, load_sem.at[4])
+    load_send2 = pltpu.make_async_copy(send2_hbm, send2_ref, load_sem.at[5])
+    load_list2 = pltpu.make_async_copy(list2_hbm, list2_ref, load_sem.at[6])
+    load_list3 = pltpu.make_async_copy(list3_hbm, list3_ref, load_sem.at[7])
+    load_send1.start()
+    load_send2.start()
+    load_list2.start()
+    load_list3.start()
     load_maps = pltpu.make_async_copy(maps_hbm, maps, load_sem.at[1])
     load_maps.start()
     lax.fori_loop(1, NCOL, hello, 0)
@@ -80,6 +88,7 @@
     load_list.start()
     load_trans.start()
 
+    load_send1.wait()
     who = send1_ref[...].T
     lane = iota((GH1, B1), 1)
     load_one.wait()
@@ -109,6 +118,7 @@
     for c in range(8):
         total = total + dot_nt(children[c * B2 : (c + 1) * B2], maps[c])
     two = total.astype(BF)
+    load_send2.wait()
     who = send2_ref[...].T
     lane = iota((GH2, B2), 1)
     pick = jnp.concatenate([hot(who[:, p : p + 1] == lane) for p in range(NROW)], axis=0)
@@ -201,6 +211,8 @@
     for o in range(0, NOFF, 2):
         tcat[:, o * D : (o + 2) * D] = jnp.concatenate([trans[o], trans[o + 1]], axis=1)
 
+    load_list2.wait()
+    load_list3.wait()
     list2 = list2_ref[...]
     entries3 = as_row(list3_ref[...], B3)
     entries3 = entries3 + (entries3 & -8)
@@ -234,7 +246,9 @@
         return 0
 
     lax.fori_loop(0, SLOTS, chunks(far, SLOTS), 0)
-    out1_ref[...] = dot(tcat[...], g[:, 0:B1])
+    far1[...] = dot(tcat[...], g[:, 0:B1])
+    save = pltpu.make_async_copy(far1, out1_ref, load_sem.at[8])
+    save.start()
 
     pltpu.make_async_copy(ghost2.at[0 : NROW - 1], ghost2.at[0 : NROW - 1], recv_sem.at[1]).wait()
     tab2 = turned(jnp.concatenate([two, ghost2[...].reshape(NROW * GH2, D)], axis=0))
@@ -249,6 +263,7 @@
     out2_ref[...] = 0.5 * both[0:B2]
     out3_ref[...] = 0.25 * both[B2 : B2 + B3]
 
+    save.wait()
     pltpu.make_async_copy(send1.at[0 : NCOL - 1], send1.at[0 : NCOL - 1], send_sem.at[0]).wait()
     pltpu.make_async_copy(send2.at[0 : NROW - 1], send2.at[0 : NROW - 1], send_sem.at[1]).wait()
 
@@ -271,8 +286,8 @@
     found = pl.pallas_call(
         kernel,
         out_shape=shapes,
-        in_specs=[any_, vmem, any_, vmem, vmem, vmem, any_, any_],
-        out_specs=(vmem, vmem, vmem),
+        in_specs=[pl.BlockSpec(memory_space=pltpu.HBM)] * 8,
+        out_specs=(any_, vmem, vmem),
         scratch_shapes=[
             pltpu.VMEM((D, B1), BF),
             pltpu.VMEM((NOFF, B1), jnp.int32),
@@ -285,7 +300,12 @@
             pltpu.VMEM((NROW, GH2, D), BF),
             pltpu.VMEM((NOFF * D, B1 + 128), BF),
             pltpu.VMEM((D, NCOL * GH1), BF),
-            pltpu.SemaphoreType.DMA((4,)),
+            pltpu.VMEM((NCOL, GH1), jnp.int32),
+            pltpu.VMEM((NROW, GH2), jnp.int32),
+            pltpu.VMEM((NOFF, B2), jnp.int32),
+            pltpu.VMEM((B3, NOFF), jnp.int32),
+            pltpu.VMEM((D, B1), F32),
+            pltpu.SemaphoreType.DMA((9,)),
             pltpu.SemaphoreType.DMA((2,)),
             pltpu.SemaphoreType.DMA((2,)),
             pltpu.SemaphoreType.REGULAR,

time: 36.8 us -> 36.1 us (0.981)
  Pallas kernels: 36 us -> 35.4 us
    pallas_call x1, Pallas kernels: 34.1 us -> 33.5 us  [on_device(): pl.pallas_call(kernel, out_shape=shapes, in_specs=[pl.BlockSpec(memory_sp...]
where the time goes in v6:
time: 36.1 us; the launch traced here: 36 us
  Pallas kernels  35.4 us (98%)
  between operations  0.64 us (2%)
    pallas_call x1, Pallas kernels, on_device(): pl.pallas_call(kernel, out_shape=shapes, in_specs=[pl.BlockSpec(memory_sp...  33.5 us
    pallas_call x1, Pallas kernels, on_device(): pl.pallas_call(pass_on, out_shape=shapes, in_specs=[vmem] * 3, out_specs=...  1.82 us

profile of v6, /device:TPU:1, one launch (start us, length us, event | category | flops | bytes accessed | tf_op | source)
XLA Modules:
  0.0 36.0 jit_solution(1359352356972242590)
XLA Ops:
  0.6 33.5 %shard_map.103 = (f32[192,512]{1,0:T(8,128)}, f32[64,192]{1,0:T(8,128)}, f32[8,192]{1,0:T(8,128)}) custom-call(bf16[192,512]{1,0:T(8,128)(2,1)} %one_hbm.1, s32[32,32]{1,0:T(8,128)} %bitcast.7, s32[32,512]{1,0:T(8,128)} %bitcast.6, s32[16,16]{1,0:T(8,128)} %bitcast.9, s32[32,64]{1,0:T(8,128)} %bitcast.8, s32[8,32]{1,0:T(8,128)} %list3_hbm.1, ...), custom_call_target="tpu_custom_call" | custom-call | tf_op jit(solution)/shard_map/pallas_call | solution.py:286
  34.2 1.8 %shard_map.104 = (f32[192,512]{1,0:T(8,128)}, f32[64,192]{1,0:T(8,128)}, f32[8,192]{1,0:T(8,128)}) custom-call(f32[192,512]{1,0:T(8,128)} %get-tuple-element.9.refs_0_, f32[64,192]{1,0:T(8,128)} %get-tuple-element.10.refs_1_, f32[8,192]{1,0:T(8,128)} %get-tuple-element.11.refs_2_), custom_call_target="tpu_custom_call" | custom-call | tf_op jit(solution)/shard_map/pallas_call | solution.py:321
